TPU v7x, 32 devices: a whole 2x2x4 slice. The times are simulated.
32 devices in a mesh: groups: 2 (over x), expert: 16 (over z, y, core).
Axes of the slice: x: 2, y: 2, z: 4, core: 2. Of those that a mesh axis runs over, the one named last changes fastest.
Arguments:
- tokens: bfloat16 [4096, 1664], P(('groups', 'expert')), parts along dimension 0, may hold values from -6 to 6
- gate_probs: float32 [4096, 2], P(('groups', 'expert')), parts along dimension 0, may hold values from 0.1 to 1
- expert_ids: int32 [4096, 2], P(('groups', 'expert')), parts along dimension 0, may hold values from 0 to 3, all different within a row; in each aligned block of 128 rows (0 to 127, 128 to 255, ...) at most 65 rows name the same one
- priority: int32 [4096], P(('groups', 'expert')), parts along dimension 0, may hold values from 0 to 2047, each once
- weight_in: bfloat16 [16, 1664, 1024], P('expert'), may hold values from -0.15625 to 0.15625
- weight_out: bfloat16 [16, 1024, 1664], P('expert'), may hold values from -0.09375 to 0.09375
Outputs:
- combined: bfloat16 [4096, 1664], P(('groups', 'expert')), parts along dimension 0
There are 2 independent parts, one for each index of `groups`. A program takes and returns all parts, laid end to end along the dimension named above; an argument that names none is the same for every part. Nothing has to cross between parts.
Inputs may be any that keep to these rules, and one draw needn't show every extreme that they name: `expert_ids`: in the rows of one device no expert is named by more than 65 rows over both columns; some expert reaches 65 in some device's rows. `priority`: each value occurs once in a group.
All inputs are finite; a program needn't handle non-finite values.
Results may differ from a plain program's by a relative error of at most 0.0065.
Values may be sent and summed in bfloat16 or wider, within the bound.
A program may use at most 128 MiB of HBM per device.

v0:
```python
import jax
import jax.numpy as jnp
from jax import lax
from jax.sharding import PartitionSpec as P


def place_rows(assigned, kept_mask, tokens, n_experts, most):
    tok_rows = tokens.shape[0]
    count_all = assigned.shape[0]
    one_hot = (assigned[:, None] == jnp.arange(n_experts, dtype=jnp.int32)[None, :]).astype(
        jnp.int32
    )
    position = jnp.sum((jnp.cumsum(one_hot, 0) - one_hot) * one_hot, 1)
    slot_index = assigned * most + position
    slot_hot = (
        (slot_index[:, None] == jnp.arange(n_experts * most, dtype=jnp.int32)[None, :])
        & kept_mask[:, None]
    ).astype(jnp.bfloat16)
    owner = jnp.arange(count_all, dtype=jnp.int32) % tok_rows
    token_hot = (owner[:, None] == jnp.arange(tok_rows, dtype=jnp.int32)[None, :]).astype(
        jnp.bfloat16
    )
    dispatch_map = jnp.einsum(
        "as,at->st", slot_hot, token_hot, preferred_element_type=jnp.float32
    ).astype(jnp.bfloat16)
    packed = jnp.dot(dispatch_map, tokens, preferred_element_type=jnp.float32).astype(jnp.bfloat16)
    return (packed.reshape(n_experts, most, tokens.shape[1]), slot_index)


def return_sums(partial_value):
    sources, rows, width = partial_value.shape
    back = lax.all_to_all(partial_value, "expert", split_axis=0, concat_axis=0, tiled=True)
    summed = jnp.sum(back.astype(jnp.float32).reshape(sources // 4, 4, rows, width), 1)
    return summed.astype(jnp.bfloat16)


def expert_pass(packed, weight_in, weight_out):
    first_proj = weight_in[0]
    second_proj = weight_out[0]
    n_experts, most, model_width = packed.shape
    sending = jnp.repeat(packed, 4, axis=0)
    arrived = lax.all_to_all(sending, "expert", split_axis=0, concat_axis=0, tiled=True)
    flat = arrived.reshape(-1, arrived.shape[2])
    hidden = jax.nn.gelu(
        jnp.dot(flat, first_proj, preferred_element_type=jnp.float32), approximate=False
    ).astype(jnp.bfloat16)
    partial_value = jnp.dot(hidden, second_proj, preferred_element_type=jnp.float32).astype(
        jnp.bfloat16
    )
    summed = return_sums(partial_value.reshape(arrived.shape))
    return summed.reshape(n_experts * most, model_width)


def shards(tokens, gate_probs, expert_ids, priority, weight_in, weight_out):
    tok_rows = tokens.shape[0]
    n_experts = lax.axis_size("expert") // 4
    most = 2 * tok_rows // n_experts + 1
    capacity = 2 * tok_rows * lax.axis_size("expert") // n_experts
    first_ids = expert_ids[:, 0]
    second_ids = expert_ids[:, 1]
    portion_ranks = lax.all_gather(priority, "expert", axis=0, tiled=True)
    portion_ids = lax.all_gather(expert_ids, "expert", axis=0, tiled=True)
    earlier = portion_ranks[None, :] < priority[:, None]
    portion_first = portion_ids[:, 0][None, :]
    portion_second = portion_ids[:, 1][None, :]
    before_first = jnp.sum(((portion_first == first_ids[:, None]) & earlier).astype(jnp.int32), 1)
    total_first = jnp.sum((portion_first == second_ids[:, None]).astype(jnp.int32), 1)
    before_second = jnp.sum(
        ((portion_second == second_ids[:, None]) & earlier).astype(jnp.int32), 1
    )
    before_first, total_first, before_second = (before_first, total_first, before_second)
    kept_first = before_first < capacity
    kept_second = jnp.minimum(total_first, capacity) + before_second < capacity
    weight_first = jnp.where(kept_first, gate_probs[:, 0], jnp.float32(0.0))
    weight_second = jnp.where(kept_second, gate_probs[:, 1], jnp.float32(0.0))
    combined = jnp.zeros(tokens.shape, jnp.float32)
    for column, kept_mask, weighting in (
        (first_ids, kept_first, weight_first),
        (second_ids, kept_second, weight_second),
    ):
        packed, slot_index = place_rows(column, kept_mask, tokens, n_experts, most)
        outputs = expert_pass(packed, weight_in, weight_out)
        combined = combined + weighting[:, None] * jnp.take(outputs, slot_index, axis=0).astype(
            jnp.float32
        )
    return combined.astype(jnp.bfloat16)


def solution(mesh):
    placed = (
        P(("groups", "expert"), None),
        P(("groups", "expert"), None),
        P(("groups", "expert"), None),
        P(("groups", "expert")),
        P("expert", None, None),
        P("expert", None, None),
    )
    return jax.shard_map(
        shards, mesh=mesh, in_specs=placed, out_specs=P(("groups", "expert"), None), check_vma=False
    )
```

profile of v0, /device:TPU:8, one launch (start us, length us, event | category | flops | bytes accessed | tf_op | source)
XLA Modules:
  0.0 431.4 jit_solution(7415612148618374377)
XLA Ops:
  0.0 0.0 copy-start
  0.0 0.8 slice_bitcast_fusion.1
  0.9 0.0 copy-start.2
  0.9 0.0 copy-start.3
  0.9 19.2 %all_gather.6 = s32[2048,2]{0,1:T(2,128)S(1)} all-gather(s32[128,2]{0,1:T(2,128)} %param.10), channel_id=1, replica_groups=mesh['groups'=2,'expert'=16] {'expert'}, dimensions={0}, use_global_device_ids=true | all-gather | bytes 17408 | tf_op jit(solution)/shard_map/all_gather | solution.py:62
  20.1 0.5 and_select_fusion
  20.6 0.6 fusion.54
  21.2 17.5 %all-gather = s32[16,1,128]{2,1,0:T(1,128)S(1)} all-gather(s32[1,1,128]{2,1,0:T(1,128)} %bitcast.69), channel_id=1, replica_groups=mesh['groups'=2,'expert'=16] {'expert'}, dimensions={0}, use_global_device_ids=true | all-gather | bytes 8704 | tf_op jit(solution)/shard_map/all_gather | solution.py:61
  38.6 0.1 fusion.45
  38.7 0.0 copy-done.2
  38.7 0.0 copy-done.3
  38.8 0.7 fusion.44
  39.5 0.2 reduce_window_sum.17
  39.6 1.0 reduce_window_sum.18
  40.6 0.8 select_reduce_fusion
  41.5 0.0 copy-start.4
  41.5 0.0 copy-start.6
  41.5 0.6 copy-done.4
  42.1 0.8 fusion.53
  42.9 0.0 copy-done.6
  42.9 1.3 convert_reduce_fusion.2
  44.2 0.8 fusion.51
  44.9 2.6 convolution_convert_fusion.2
  47.6 2.4 reshape.102
  49.9 3.3 broadcast_in_dim.20
  53.2 0.0 copy-start.8
  53.2 7.7 %all-to-all-start.2 = ((bf16[16,65,1664]{2,1,0:T(8,128)(2,1)}), bf16[16,65,1664]{2,1,0:T(8,128)(2,1)}, u32[]{:S(2)}, u32[]{:S(2)}) async-start(bf16[16,65,1664]{2,1,0:T(8,128)(2,1)} %bitcast.64), calls=%async_computation.2 | async-start | bytes 7667712 | tf_op jit(solution)/shard_map/all_to_all | solution.py:42
  60.9 0.0 copy-done.8
  60.9 2.7 convolution_convert_fusion.3
  63.6 2.4 reshape.96
  65.9 78.1 %all-to-all-done.2 = bf16[16,65,1664]{2,1,0:T(8,128)(2,1)} async-done(((bf16[16,65,1664]{2,1,0:T(8,128)(2,1)}), bf16[16,65,1664]{2,1,0:T(8,128)(2,1)}, u32[]{:S(2)}, u32[]{:S(2)}) %all-to-all-start.2) | async-done | bytes 3461152 | tf_op jit(solution)/shard_map/all_to_all | solution.py:42
  144.0 3.3 broadcast_in_dim.19
  147.3 6.6 %all-to-all-start = ((bf16[16,65,1664]{2,1,0:T(8,128)(2,1)}), bf16[16,65,1664]{2,1,0:T(8,128)(2,1)}, u32[]{:S(2)}, u32[]{:S(2)}) async-start(bf16[16,65,1664]{2,1,0:T(8,128)(2,1)} %bitcast.65), calls=%async_computation | async-start | bytes 7667712 | tf_op jit(solution)/shard_map/all_to_all | solution.py:42
  153.9 3.9 reshape.104
  157.8 15.3 %fusion.5 = bf16[1040,1024]{1,0:T(8,128)(2,1)S(1)} fusion(bf16[1040,1664]{1,0:T(8,128)(2,1)} %reshape.104, bf16[1,1664,1024]{2,1,0:T(8,128)(2,1)} %param.12), kind=kOutput, calls=%fused_computation.11 | convolution fusion | flops 3613409280 | bytes 8998912 | tf_op jit(solution)/shard_map/dot_general | solution.py:45
  173.1 0.0 copy-done
  173.1 5.4 %convolution_convert_fusion = bf16[1040,1664]{1,0:T(8,128)(2,1)} fusion(bf16[1040,1024]{1,0:T(8,128)(2,1)S(1)} %fusion.5, bf16[1,1024,1664]{2,1,0:T(8,128)(2,1)S(1)} %copy-done), kind=kOutput, calls=%fused_computation.2 | convolution fusion | flops 3545917440 | bytes 8998912 | tf_op jit(solution)/shard_map/dot_general | solution.py:47
  178.5 4.0 reshape.105
  182.5 54.5 %all-to-all-done = bf16[16,65,1664]{2,1,0:T(8,128)(2,1)} async-done(((bf16[16,65,1664]{2,1,0:T(8,128)(2,1)}), bf16[16,65,1664]{2,1,0:T(8,128)(2,1)}, u32[]{:S(2)}, u32[]{:S(2)}) %all-to-all-start) | async-done | bytes 3461152 | tf_op jit(solution)/shard_map/all_to_all | solution.py:42
  237.0 6.6 %all-to-all-start.3 = ((bf16[16,65,1664]{2,1,0:T(8,128)(2,1)}), bf16[16,65,1664]{2,1,0:T(8,128)(2,1)}, u32[]{:S(2)}, u32[]{:S(2)}) async-start(bf16[16,65,1664]{2,1,0:T(8,128)(2,1)} %reshape.105), calls=%async_computation.3 | async-start | bytes 7667712 | tf_op jit(solution)/shard_map/all_to_all | solution.py:32
  243.5 3.9 reshape.98
  247.4 15.3 %fusion.2 = bf16[1040,1024]{1,0:T(8,128)(2,1)S(1)} fusion(bf16[1040,1664]{1,0:T(8,128)(2,1)} %reshape.98, bf16[1,1664,1024]{2,1,0:T(8,128)(2,1)} %param.12), kind=kOutput, calls=%fused_computation.8 | convolution fusion | flops 3613409280 | bytes 8998912 | tf_op jit(solution)/shard_map/dot_general | solution.py:45
  262.7 5.4 %convolution_convert_fusion.1 = bf16[1040,1664]{1,0:T(8,128)(2,1)} fusion(bf16[1040,1024]{1,0:T(8,128)(2,1)S(1)} %fusion.2, bf16[1,1024,1664]{2,1,0:T(8,128)(2,1)S(1)} %copy-done), kind=kOutput, calls=%fused_computation.3 | convolution fusion | flops 3545917440 | bytes 8998912 | tf_op jit(solution)/shard_map/dot_general | solution.py:47
  268.1 3.9 reshape.99
  272.0 0.0 copy-start.1
  272.0 0.0 copy-start.5
  272.0 0.0 copy-start.7
  272.0 54.6 %all-to-all-done.3 = bf16[16,65,1664]{2,1,0:T(8,128)(2,1)} async-done(((bf16[16,65,1664]{2,1,0:T(8,128)(2,1)}), bf16[16,65,1664]{2,1,0:T(8,128)(2,1)}, u32[]{:S(2)}, u32[]{:S(2)}) %all-to-all-start.3) | async-done | bytes 3461152 | tf_op jit(solution)/shard_map/all_to_all | solution.py:32
  326.6 6.6 %all-to-all-start.1 = ((bf16[16,65,1664]{2,1,0:T(8,128)(2,1)}), bf16[16,65,1664]{2,1,0:T(8,128)(2,1)}, u32[]{:S(2)}, u32[]{:S(2)}) async-start(bf16[16,65,1664]{2,1,0:T(8,128)(2,1)} %reshape.99), calls=%async_computation.1 | async-start | bytes 7667712 | tf_op jit(solution)/shard_map/all_to_all | solution.py:32
  333.2 0.0 copy-done.1
  333.2 0.0 copy-done.5
  333.2 0.0 copy-done.7
  333.2 3.9 bitcast_reduce_fusion
  337.2 2.4 convert_element_type.85
  339.5 76.8 %all-to-all-done.1 = bf16[16,65,1664]{2,1,0:T(8,128)(2,1)} async-done(((bf16[16,65,1664]{2,1,0:T(8,128)(2,1)}), bf16[16,65,1664]{2,1,0:T(8,128)(2,1)}, u32[]{:S(2)}, u32[]{:S(2)}) %all-to-all-start.1) | async-done | bytes 3461152 | tf_op jit(solution)/shard_map/all_to_all | solution.py:32
  416.3 3.9 bitcast_reduce_fusion.1
  420.2 2.4 convert_element_type.75
  422.6 3.3 gather_fusion.1
  425.9 3.3 gather_fusion
  429.2 2.2 add_convert_fusion
  (4 shorter events, 0.0 us)
Async XLA Ops:
  0.0 173.1 %copy-start = (bf16[1,1024,1664]{2,1,0:T(8,128)(2,1)S(1)}, bf16[1,1024,1664]{2,1,0:T(8,128)(2,1)}, u32[]{:S(2)}) copy-start(bf16[1,1024,1664]{2,1,0:T(8,128)(2,1)} %param.13) | copy-start | bytes 10223620
  0.9 37.9 %copy-start.2 = (s32[128]{0:T(128)}, s32[128]{0:T(128)S(1)}, u32[]{:S(2)}) copy-start(s32[128]{0:T(128)S(1)} %get-tuple-element.22) | copy-start | bytes 1540
  0.9 37.9 %copy-start.3 = (s32[128]{0:T(128)}, s32[128]{0:T(128)S(1)}, u32[]{:S(2)}) copy-start(s32[128]{0:T(128)S(1)} %get-tuple-element.23) | copy-start | bytes 1540
  41.5 0.6 copy-start.4
  41.5 1.3 copy-start.6
  53.2 7.7 %copy-start.8 = (s32[128]{0:T(128)S(1)}, s32[128]{0:T(128)}, u32[]{:S(2)}) copy-start(s32[128]{0:T(128)} %and_select_fusion) | copy-start | bytes 1540
  53.2 90.8 %all-to-all-start.2 = ((bf16[16,65,1664]{2,1,0:T(8,128)(2,1)}), bf16[16,65,1664]{2,1,0:T(8,128)(2,1)}, u32[]{:S(2)}, u32[]{:S(2)}) async-start(bf16[16,65,1664]{2,1,0:T(8,128)(2,1)} %bitcast.64), calls=%async_computation.2 | async-start | bytes 7667712 | tf_op jit(solution)/shard_map/all_to_all | solution.py:42
  147.3 89.7 %all-to-all-start = ((bf16[16,65,1664]{2,1,0:T(8,128)(2,1)}), bf16[16,65,1664]{2,1,0:T(8,128)(2,1)}, u32[]{:S(2)}, u32[]{:S(2)}) async-start(bf16[16,65,1664]{2,1,0:T(8,128)(2,1)} %bitcast.65), calls=%async_computation | async-start | bytes 7667712 | tf_op jit(solution)/shard_map/all_to_all | solution.py:42
  237.0 89.7 %all-to-all-start.3 = ((bf16[16,65,1664]{2,1,0:T(8,128)(2,1)}), bf16[16,65,1664]{2,1,0:T(8,128)(2,1)}, u32[]{:S(2)}, u32[]{:S(2)}) async-start(bf16[16,65,1664]{2,1,0:T(8,128)(2,1)} %reshape.105), calls=%async_computation.3 | async-start | bytes 7667712 | tf_op jit(solution)/shard_map/all_to_all | solution.py:32
  272.0 61.2 %copy-start.1 = (s32[128,2]{0,1:T(2,128)S(1)}, s32[128,2]{0,1:T(2,128)}, u32[]{:S(2)}) copy-start(s32[128,2]{0,1:T(2,128)} %param.10) | copy-start | bytes 3076
  272.0 61.2 %copy-start.5 = (s32[128]{0:T(128)S(1)}, s32[128]{0:T(128)}, u32[]{:S(2)}) copy-start(s32[128]{0:T(128)} %copy-done.4) | copy-start | bytes 1540
  272.0 61.2 %copy-start.7 = (s32[128]{0:T(128)S(1)}, s32[128]{0:T(128)}, u32[]{:S(2)}) copy-start(s32[128]{0:T(128)} %copy-done.6) | copy-start | bytes 1540
  326.6 89.7 %all-to-all-start.1 = ((bf16[16,65,1664]{2,1,0:T(8,128)(2,1)}), bf16[16,65,1664]{2,1,0:T(8,128)(2,1)}, u32[]{:S(2)}, u32[]{:S(2)}) async-start(bf16[16,65,1664]{2,1,0:T(8,128)(2,1)} %reshape.99), calls=%async_computation.1 | async-start | bytes 7667712 | tf_op jit(solution)/shard_map/all_to_all | solution.py:32
where the time goes:
time: 434 us; the launch traced here: 431 us
  waiting for transfers between devices  264 us (61%)
  matrix products  46.7 us (11%)
  local copies, waits for them, and re-layouts  40.5 us (9%)
  blocking collectives  36.7 us (8%)
  starting transfers between devices  27.3 us (6%)
  other arithmetic  16.2 us (4%)
    all_to_all x2, waiting for transfers between devices, expert_pass(): lax.all_to_all(sending, 'expert', split_axis=0, concat_axis=0, tiled=True)  133 us
    all_to_all x2, waiting for transfers between devices, return_sums(): lax.all_to_all(partial_value, 'expert', split_axis=0, concat_axis=0, tile...  131 us
    dot_general x2, matrix products, expert_pass(): jnp.dot(flat, first_proj, preferred_element_type=jnp.float32)  30.6 us
    all_gather x1, blocking collectives, shards(): portion_ids = lax.all_gather(expert_ids, 'expert', axis=0, tiled=True)  19.2 us
    all_gather x1, blocking collectives, shards(): portion_ranks = lax.all_gather(priority, 'expert', axis=0, tiled=True)  17.5 us
    all_to_all x2, starting transfers between devices, expert_pass(): lax.all_to_all(sending, 'expert', split_axis=0, concat_axis=0, tiled=True)  14.2 us
    all_to_all x2, starting transfers between devices, return_sums(): lax.all_to_all(partial_value, 'expert', split_axis=0, concat_axis=0, tile...  13.1 us
    dot_general x2, matrix products, expert_pass(): jnp.dot(hidden, second_proj, preferred_element_type=jnp.float32)  10.8 us
  transfers between devices with their start and end apart: 4, of which 4 were waited for; matrix products, arithmetic and copies ran while one was open for 16% of the time, Pallas kernels for 0%

commit v1 on v0

v1 whole, which is shorter than its diff:
```python
import functools

import jax
import jax.numpy as jnp
from jax import lax
from jax.experimental import pallas as pl
from jax.experimental.pallas import tpu as pltpu
from jax.sharding import PartitionSpec as P

F32 = jnp.float32
BF16 = jnp.bfloat16


def gelu(x):
    return 0.5 * x * (1.0 + lax.erf(x * 0.7071067811865476))


def kernel(
    n_exp, base, tok, width,
    tokens, gates, ids, rank_col, meta, w_in, w_out,
    out,
    w1, w2, snd, rows, xs, hs, ext_in, ext_out, give, got, keep, ysend, ygot, rsend, ret, info, acc,
    w_sem, z_s, z_r, fs_s, fs_r, fy_s, fy_r, ff_s, ff_r, g_s, g_r, y_s, y_r, r_s, r_r,
    mz_s, mz_r, mp_s, mp_r,
):
    tiles = width // 128
    tail = tiles * base
    me = lax.axis_index("expert")
    plane, col = me // 4, me % 4
    sibling = plane * 4 + (col // 2) * 2 + (col + 1) % 2
    across = plane * 4 + (col + 2) % 4

    def peer(j):
        return ((plane + j) % n_exp) * 4 + col

    def remote(src, dst, send, recv, dev):
        return pltpu.make_async_remote_copy(
            src_ref=src, dst_ref=dst, send_sem=send, recv_sem=recv,
            device_id={"expert": dev}, device_id_type=pl.DeviceIdType.MESH,
        )

    def dispatch(j):
        return remote(snd.at[j], rows.at[0, j], z_s.at[j], z_r.at[j], peer(n_exp - j))

    def to_sibling(d):
        return remote(rows.at[0, d], rows.at[1, d], fs_s.at[d], fs_r.at[d], sibling)

    def to_across(d):
        return remote(rows.at[0, d], rows.at[2, d], fy_s.at[d], fy_r.at[d], across)

    def pass_on(d):
        return remote(rows.at[2, d], rows.at[3, d], ff_s.at[d], ff_r.at[d], sibling)

    def give_copy(d):
        return remote(give.at[d], got.at[d], g_s.at[d], g_r.at[d], sibling)

    def pair_copy(d):
        return remote(ysend.at[d], ygot.at[d], y_s.at[d], y_r.at[d], across)

    def return_copy(d):
        return remote(
            rsend.at[d], ret.at[n_exp - d], r_s.at[d], r_r.at[n_exp - d], peer(d)
        )

    def info_copy(j):
        return remote(info.at[0, 0], info.at[0, j], mz_s.at[j], mz_r.at[j], peer(n_exp - j))

    def info_sibling():
        return remote(info.at[0], info.at[1], mp_s.at[0], mp_r.at[0], sibling)

    def info_across():
        return remote(
            info.at[pl.ds(0, 2)], info.at[pl.ds(2, 2)], mp_s.at[1], mp_r.at[1], across
        )

    load_in = pltpu.make_async_copy(w_in.at[0], w1, w_sem.at[0])
    load_out = pltpu.make_async_copy(w_out.at[0], w2, w_sem.at[1])
    load_in.start()
    load_out.start()

    barrier = pltpu.get_barrier_semaphore()

    def greet(j, c):
        pl.semaphore_signal(
            barrier, inc=1, device_id={"expert": peer(j)}, device_id_type=pl.DeviceIdType.MESH
        )
        return c

    lax.fori_loop(1, n_exp, greet, 0)
    for dev in (sibling, across):
        pl.semaphore_signal(
            barrier, inc=1, device_id={"expert": dev}, device_id_type=pl.DeviceIdType.MESH
        )

    info[0, 0] = meta[...]
    ext_in[...] = jnp.zeros_like(ext_in)
    ext_out[...] = jnp.zeros_like(ext_out)
    first_row, second_row = meta[1:2, :], meta[2:3, :]
    upper = (
        lax.broadcasted_iota(jnp.int32, (tok, tok), 0)
        < lax.broadcasted_iota(jnp.int32, (tok, tok), 1)
    ).astype(BF16)
    slot_iota = lax.broadcasted_iota(jnp.int32, (base + 16, tok), 0).astype(F32)

    def pack(expert, dst):
        hit = ((first_row == expert) | (second_row == expert)).astype(F32)
        hit8 = jnp.broadcast_to(hit, (8, tok))
        place = jnp.dot(hit8.astype(BF16), upper, preferred_element_type=F32)[0:1, :]
        pick = jnp.where(slot_iota == place, hit, 0.0).astype(BF16)
        packed = jnp.dot(pick, tokens[...], preferred_element_type=F32)
        for c in range(tiles):
            lanes = slice(c * 128, (c + 1) * 128)
            dst[c * base : (c + 1) * base, :] = packed[:base, lanes].astype(BF16)
            ext_out[0, c : c + 1, :] = packed[base : base + 1, lanes]
        dst[tail : tail + 16, :] = ext_out[0].astype(BF16)

    pack(plane, rows.at[0, 0])
    pl.semaphore_wait(barrier, n_exp + 1)
    to_across(0).start()
    to_sibling(0).start()

    def start_info(j, c):
        info_copy(j).start()
        return c

    lax.fori_loop(1, n_exp, start_info, 0)

    def pack_send(j, c):
        pack((plane + n_exp - j) % n_exp, snd.at[j])
        dispatch(j).start()
        return c

    lax.fori_loop(1, n_exp, pack_send, 0)

    def wait_info(j, c):
        info_copy(j).wait_recv()
        return c

    lax.fori_loop(1, n_exp, wait_info, 0)
    info_sibling().start()
    info_sibling().wait_recv()
    info_across().start()
    load_in.wait()
    load_out.wait()

    order = (1, 3, 0, 2)

    def finish(d):
        pair_copy(d).wait_recv()
        rsend[d] = (keep[d, 0] + ygot[d].astype(F32)).astype(BF16)

    def group(d, c):
        @pl.when(d > 0)
        def _():
            dispatch(d).wait_recv()
            to_across(d).start()
            to_sibling(d).start()

        to_across(d).wait_recv()
        pass_on(d).start()
        to_sibling(d).wait_recv()
        pass_on(d).wait_recv()
        for i, rel in enumerate(order):
            last = rows[rel, d, tail : tail + 16, :].astype(F32)
            for t in range(tiles):
                lanes = slice(t * 128, (t + 1) * 128)
                xs[i * base : (i + 1) * base, lanes] = rows[rel, d, t * base : (t + 1) * base, :]
                ext_in[i : i + 1, lanes] = last[t : t + 1, :]
        xs[4 * base :, :] = ext_in[...].astype(BF16)
        hid = w1.shape[1]
        for n in range(0, hid, 256):
            h = jnp.dot(xs[...], w1[:, n : n + 256], preferred_element_type=F32)
            hs[:, n : n + 256] = gelu(h).astype(BF16)
        for n in range(0, width, 256):
            wide = min(256, width - n)
            p = jnp.dot(hs[...], w2[:, n : n + wide], preferred_element_type=F32)
            for t in range(n // 128, (n + wide) // 128):
                q = p[:, t * 128 - n : (t + 1) * 128 - n]
                span = slice(t * base, (t + 1) * base)
                give[d, 0, span, :] = q[:base].astype(BF16)
                give[d, 1, span, :] = q[base : 2 * base].astype(BF16)
                keep[d, 0, span, :] = q[2 * base : 3 * base]
                keep[d, 1, span, :] = q[3 * base : 4 * base]
                for i in range(4):
                    ext_out[i, t : t + 1, :] = q[4 * base + i : 4 * base + i + 1]
        for i in range(2):
            give[d, i, tail : tail + 16, :] = ext_out[i].astype(BF16)
            keep[d, i, tail : tail + 16, :] = ext_out[2 + i]
        give_copy(d).start()

        @pl.when(d > 0)
        def _():
            finish(d - 1)

        @pl.when(d > 1)
        def _():
            return_copy(d - 1).start()

        give_copy(d).wait_recv()
        ysend[d] = (keep[d, 1] + got[d, 1].astype(F32)).astype(BF16)
        pair_copy(d).start()
        keep[d, 0] = keep[d, 0] + got[d, 0].astype(F32)
        return c

    lax.fori_loop(0, n_exp, group, 0)

    info_across().wait_recv()
    mine, first, second = rank_col[...], ids[:, 0:1], ids[:, 1:2]

    def count(m, sums):
        r, k = m // n_exp, m % n_exp
        block = info[r, k]
        ahead = block[0:1, :] < mine
        one, two = block[1:2, :], block[2:3, :]
        a, b, c = sums
        a = a + jnp.where((one == first) & ahead, 1.0, 0.0)
        b = b + jnp.where(one == second, 1.0, 0.0)
        c = c + jnp.where((two == second) & ahead, 1.0, 0.0)
        return a, b, c

    zero = jnp.zeros((tok, tok), F32)
    sums = lax.fori_loop(0, 4 * n_exp, count, (zero, zero, zero))
    before_first, total_first, before_second = [jnp.sum(v, axis=1, keepdims=True) for v in sums]
    capacity = float(8 * tok)
    weight_first = jnp.where(before_first < capacity, gates[:, 0:1], 0.0)
    weight_second = jnp.where(
        jnp.minimum(total_first, capacity) + before_second < capacity, gates[:, 1:2], 0.0
    )
    lower = (
        lax.broadcasted_iota(jnp.int32, (tok, tok), 1)
        < lax.broadcasted_iota(jnp.int32, (tok, tok), 0)
    ).astype(BF16)
    lane = lax.broadcasted_iota(jnp.int32, (tok, tok), 1).astype(F32)

    def combine(expert, block):
        one, two = first == expert, second == expert
        hit = jnp.where(one | two, 1.0, 0.0)
        weight = jnp.where(one, weight_first, jnp.where(two, weight_second, 0.0))
        place = jnp.dot(
            lower, jnp.broadcast_to(hit, (tok, tok)).astype(BF16), preferred_element_type=F32
        )
        pick = jnp.where(place == lane, hit, 0.0).astype(BF16)[:, :base]
        over = jnp.where(place[:, 0:1] == float(base), weight, 0.0) * hit
        last = block[tail : tail + 16, :].astype(F32)
        values = jnp.concatenate(
            [block[t * base : (t + 1) * base, :] for t in range(tiles)], axis=1
        )
        found = jnp.dot(pick, values, preferred_element_type=F32)
        for t in range(tiles):
            lanes = slice(t * 128, (t + 1) * 128)
            acc[:, lanes] += weight * found[:, lanes] + over * last[t : t + 1, :]

    acc[...] = jnp.zeros_like(acc)
    combine(plane, rsend.at[0])
    finish(n_exp - 1)
    return_copy(n_exp - 1).start()

    def collect(i, c):
        j = n_exp - i
        return_copy(i).wait_recv()
        combine((plane + j) % n_exp, ret.at[j])
        return c

    lax.fori_loop(1, n_exp, collect, 0)
    out[...] = acc[...].astype(BF16)

    def drain(d, c):
        to_across(d).wait_send()
        to_sibling(d).wait_send()
        pass_on(d).wait_send()
        give_copy(d).wait_send()
        pair_copy(d).wait_send()

        @pl.when(d > 0)
        def _():
            dispatch(d).wait_send()
            info_copy(d).wait_send()
            return_copy(d).wait_send()

        return c

    lax.fori_loop(0, n_exp, drain, 0)
    info_sibling().wait_send()
    info_across().wait_send()


def shards(tokens, gate_probs, expert_ids, priority, weight_in, weight_out):
    tok, width = tokens.shape
    n_exp = lax.axis_size("expert") // 4
    base = 2 * tok // n_exp
    hid = weight_in.shape[2]
    block = (width // 128) * base + 16
    meta = jnp.concatenate(
        [priority[None, :], expert_ids.T, jnp.zeros((5, tok), jnp.int32)], axis=0
    )
    vmem = pl.BlockSpec(memory_space=pltpu.VMEM)
    hbm = pl.BlockSpec(memory_space=pl.ANY)
    group_rows = 4 * base + 16
    dma = pltpu.SemaphoreType.DMA
    return pl.pallas_call(
        functools.partial(kernel, n_exp, base, tok, width),
        out_shape=jax.ShapeDtypeStruct((tok, width), BF16),
        in_specs=[vmem, vmem, vmem, vmem, vmem, hbm, hbm],
        out_specs=vmem,
        scratch_shapes=[
            pltpu.VMEM((width, hid), BF16),
            pltpu.VMEM((hid, width), BF16),
            pltpu.VMEM((n_exp, block, 128), BF16),
            pltpu.VMEM((4, n_exp, block, 128), BF16),
            pltpu.VMEM((group_rows, width), BF16),
            pltpu.VMEM((group_rows, hid), BF16),
            pltpu.VMEM((16, width), F32),
            pltpu.VMEM((4, 16, 128), F32),
            pltpu.VMEM((n_exp, 2, block, 128), BF16),
            pltpu.VMEM((n_exp, 2, block, 128), BF16),
            pltpu.VMEM((n_exp, 2, block, 128), F32),
            pltpu.VMEM((n_exp, block, 128), BF16),
            pltpu.VMEM((n_exp, block, 128), BF16),
            pltpu.VMEM((n_exp, block, 128), BF16),
            pltpu.VMEM((n_exp, block, 128), BF16),
            pltpu.VMEM((4, n_exp, 8, tok), jnp.int32),
            pltpu.VMEM((tok, width), F32),
            dma((2,)),
        ]
        + [dma((n_exp,))] * 16
        + [dma((2,))] * 2,
        compiler_params=pltpu.CompilerParams(
            collective_id=0, has_side_effects=True, vmem_limit_bytes=56 * 1024 * 1024
        ),
        cost_estimate=pl.CostEstimate(
            flops=4 * 8 * tok * width * hid,
            bytes_accessed=4 * width * hid,
            transcendentals=8 * tok * hid,
        ),
    )(tokens, gate_probs, expert_ids, priority[:, None], meta, weight_in, weight_out)


def solution(mesh):
    placed = (
        P(("groups", "expert"), None),
        P(("groups", "expert"), None),
        P(("groups", "expert"), None),
        P(("groups", "expert")),
        P("expert", None, None),
        P("expert", None, None),
    )
    return jax.shard_map(
        shards, mesh=mesh, in_specs=placed, out_specs=P(("groups", "expert"), None), check_vma=False
    )
```

time: 434 us -> 89.6 us (0.21)
  waiting for transfers between devices: 264 us -> 0 us
  Pallas kernels: 0 us -> 82 us
  matrix products: 46.7 us -> 0 us
  blocking collectives: 36.7 us -> 0 us
  local copies, waits for them, and re-layouts: 40.5 us -> 6.06 us
  starting transfers between devices: 27.3 us -> 0 us
  other arithmetic: 16.2 us -> 1.34 us
    all_to_all x4 -> x0, waiting for transfers between devices: 264 us -> none  [the longest x2 133 us: expert_pass(): lax.all_to_all(sending, 'expert', split_axis=0, concat_axis=0, tiled=True)]
    pallas_call x0 -> x1, Pallas kernels: none -> 82 us  [shards(): pl.pallas_call(functools.partial(kernel, n_exp, base, tok, width), out_sh...]
    dot_general x6 -> x0, matrix products: 46.7 us -> none  [the longest x2 30.6 us: expert_pass(): jnp.dot(flat, first_proj, preferred_element_type=jnp.float32)]
    all_gather x2 -> x0, blocking collectives: 36.7 us -> none  [the longest x1 19.2 us: shards(): portion_ids = lax.all_gather(expert_ids, 'expert', axis=0, tiled=True)]
    all_to_all x4 -> x0, starting transfers between devices: 27.3 us -> none  [the longest x2 14.2 us: expert_pass(): lax.all_to_all(sending, 'expert', split_axis=0, concat_axis=0, tiled=True)]
    reshape x6 -> x0, local copies, waits for them, and re-layouts: 20.4 us -> none  [the longest x2 7.87 us: expert_pass(): summed = return_sums(partial_value.reshape(arrived.shape))]
    reduce_sum x4 -> x0, other arithmetic: 10 us -> none  [the longest x2 7.83 us: return_sums(): jnp.sum(back.astype(jnp.float32).reshape(sources // 4, 4, rows, width), 1)]
    gather x2 -> x0, local copies, waits for them, and re-layouts: 6.66 us -> none  [shards(): jnp.take(outputs, slot_index, axis=0).astype(jnp.float32)]
  transfers between devices with their start and end apart: 4 -> 0, of which waited for: 4 -> 0; matrix products, arithmetic and copies ran while one was open for 16% -> 0% of each run, Pallas kernels for 0% -> 0%
where the time goes in v1:
time: 89.6 us; the launch traced here: 89.4 us
  Pallas kernels  82 us (92%)
  local copies, waits for them, and re-layouts  6.06 us (7%)
  other arithmetic  1.34 us (1%)
    pallas_call x1, Pallas kernels, shards(): pl.pallas_call(functools.partial(kernel, n_exp, base, tok, width), out_sh...  82 us
    unnamed x3, local copies, waits for them, and re-layouts  4.61 us

profile of v1, /device:TPU:8, one launch (start us, length us, event | category | flops | bytes accessed | tf_op | source)
XLA Modules:
  0.0 89.4 jit_solution(10417618563074026399)
XLA Ops:
  0.0 0.1 pad.2.clone
  0.1 1.3 %add_add_fusion.meta = s32[8,128]{1,0:T(8,128)} fusion(s32[2,128]{1,0:T(2,128)} %bitcast.3, s32[1,128]{1,0:T(1,128)} %bitcast.4, s32[8]{0:T(128)S(1)} %pad.2.clone), kind=kLoop, calls=%fused_computation | loop fusion | flops 2048 | bytes 5664 | tf_op jit(solution)/shard_map/concatenate | solution.py:293
  1.4 1.4 %copy.7.gates = f32[128,2]{1,0:T(8,128)} copy(f32[128,2]{0,1:T(2,128)} %param.7) | data formatting | bytes 2048 | tf_op args[1]
  2.8 1.4 %copy.9.rank_col = s32[128,1]{1,0:T(8,128)} copy(s32[128,1]{0,1:T(1,128)} %bitcast.5) | data formatting | bytes 1024 | tf_op jit(solution)/shard_map/broadcast_in_dim | solution.py:335
  4.2 1.4 %copy.8.ids = s32[128,2]{1,0:T(8,128)} copy(s32[128,2]{0,1:T(2,128)} %param.8) | data formatting | bytes 2048 | tf_op args[2]
  5.6 82.0 %shard_map.64 = bf16[128,1664]{1,0:T(8,128)(2,1)} custom-call(bf16[128,1664]{1,0:T(8,128)(2,1)} %tokens.1, f32[128,2]{1,0:T(8,128)} %copy.7.gates, s32[128,2]{1,0:T(8,128)} %copy.8.ids, s32[128,1]{1,0:T(8,128)} %copy.9.rank_col, s32[8,128]{1,0:T(8,128)} %add_add_fusion.meta, bf16[1,1664,1024]{2,1,0:T(8,128)(2,1)} %w_in.1, bf16[1,1024,1664]{2,1,0:T(8,128)(2,1)} %w_out.1), custom_call_target="tpu_custom_call" | custom-call | flops 6979321856 | bytes 6815744 | tf_op jit(solution)/shard_map/pallas_call | solution.py:300
  87.6 1.8 %copy.11 = bf16[128,1664]{1,0:T(8,128)(2,1)} copy(bf16[128,1664]{1,0:T(8,128)(2,1)} %shard_map.64) | data formatting | bytes 851968
  (1 shorter events, 0.0 us)

commit v2 on v1

--- a/solution.py
+++ b/solution.py
@@ -17,7 +17,7 @@
 
 def kernel(
     n_exp, base, tok, width,
-    tokens, gates, ids, rank_col, meta, w_in, w_out,
+    tokens, gates, ids, rank, w_in, w_out,
     out,
     w1, w2, snd, rows, xs, hs, ext_in, ext_out, give, got, keep, ysend, ygot, rsend, ret, info, acc,
     w_sem, z_s, z_r, fs_s, fs_r, fy_s, fy_r, ff_s, ff_r, g_s, g_r, y_s, y_r, r_s, r_r,
@@ -92,10 +92,12 @@
             barrier, inc=1, device_id={"expert": dev}, device_id_type=pl.DeviceIdType.MESH
         )
 
-    info[0, 0] = meta[...]
+    info[0, 0] = jnp.concatenate(
+        [rank[...].astype(F32), ids[...].astype(F32), gates[...], jnp.zeros((3, tok), F32)], axis=0
+    )
     ext_in[...] = jnp.zeros_like(ext_in)
     ext_out[...] = jnp.zeros_like(ext_out)
-    first_row, second_row = meta[1:2, :], meta[2:3, :]
+    first_row, second_row = ids[0:1, :], ids[1:2, :]
     upper = (
         lax.broadcasted_iota(jnp.int32, (tok, tok), 0)
         < lax.broadcasted_iota(jnp.int32, (tok, tok), 1)
@@ -127,7 +129,11 @@
 
     def pack_send(j, c):
         pack((plane + n_exp - j) % n_exp, snd.at[j])
-        dispatch(j).start()
+
+        @pl.when(j == 1)
+        def _():
+            dispatch(j).start()
+
         return c
 
     lax.fori_loop(1, n_exp, pack_send, 0)
@@ -150,14 +156,21 @@
         rsend[d] = (keep[d, 0] + ygot[d].astype(F32)).astype(BF16)
 
     def group(d, c):
-        @pl.when(d > 0)
-        def _():
-            dispatch(d).wait_recv()
-            to_across(d).start()
-            to_sibling(d).start()
-
         to_across(d).wait_recv()
         pass_on(d).start()
+
+        @pl.when(d < n_exp - 1)
+        def _():
+            dispatch(d + 1).wait_send()
+
+            @pl.when(d < n_exp - 2)
+            def _():
+                dispatch(d + 2).start()
+
+            dispatch(d + 1).wait_recv()
+            to_across(d + 1).start()
+            to_sibling(d + 1).start()
+
         to_sibling(d).wait_recv()
         pass_on(d).wait_recv()
         for i, rel in enumerate(order):
@@ -205,7 +218,8 @@
     lax.fori_loop(0, n_exp, group, 0)
 
     info_across().wait_recv()
-    mine, first, second = rank_col[...], ids[:, 0:1], ids[:, 1:2]
+    own = jnp.transpose(jnp.concatenate([info[0, 0]] * (tok // 8), axis=0))
+    mine, first, second = own[:, 0:1], own[:, 1:2], own[:, 2:3]
 
     def count(m, sums):
         r, k = m // n_exp, m % n_exp
@@ -222,9 +236,9 @@
     sums = lax.fori_loop(0, 4 * n_exp, count, (zero, zero, zero))
     before_first, total_first, before_second = [jnp.sum(v, axis=1, keepdims=True) for v in sums]
     capacity = float(8 * tok)
-    weight_first = jnp.where(before_first < capacity, gates[:, 0:1], 0.0)
+    weight_first = jnp.where(before_first < capacity, own[:, 3:4], 0.0)
     weight_second = jnp.where(
-        jnp.minimum(total_first, capacity) + before_second < capacity, gates[:, 1:2], 0.0
+        jnp.minimum(total_first, capacity) + before_second < capacity, own[:, 4:5], 0.0
     )
     lower = (
         lax.broadcasted_iota(jnp.int32, (tok, tok), 1)
@@ -233,7 +247,8 @@
     lane = lax.broadcasted_iota(jnp.int32, (tok, tok), 1).astype(F32)
 
     def combine(expert, block):
-        one, two = first == expert, second == expert
+        named = expert.astype(F32)
+        one, two = first == named, second == named
         hit = jnp.where(one | two, 1.0, 0.0)
         weight = jnp.where(one, weight_first, jnp.where(two, weight_second, 0.0))
         place = jnp.dot(
@@ -273,7 +288,6 @@
 
         @pl.when(d > 0)
         def _():
-            dispatch(d).wait_send()
             info_copy(d).wait_send()
             return_copy(d).wait_send()
 
@@ -290,9 +304,6 @@
     base = 2 * tok // n_exp
     hid = weight_in.shape[2]
     block = (width // 128) * base + 16
-    meta = jnp.concatenate(
-        [priority[None, :], expert_ids.T, jnp.zeros((5, tok), jnp.int32)], axis=0
-    )
     vmem = pl.BlockSpec(memory_space=pltpu.VMEM)
     hbm = pl.BlockSpec(memory_space=pl.ANY)
     group_rows = 4 * base + 16
@@ -300,7 +311,7 @@
     return pl.pallas_call(
         functools.partial(kernel, n_exp, base, tok, width),
         out_shape=jax.ShapeDtypeStruct((tok, width), BF16),
-        in_specs=[vmem, vmem, vmem, vmem, vmem, hbm, hbm],
+        in_specs=[vmem, vmem, vmem, vmem, hbm, hbm],
         out_specs=vmem,
         scratch_shapes=[
             pltpu.VMEM((width, hid), BF16),
@@ -318,7 +329,7 @@
             pltpu.VMEM((n_exp, block, 128), BF16),
             pltpu.VMEM((n_exp, block, 128), BF16),
             pltpu.VMEM((n_exp, block, 128), BF16),
-            pltpu.VMEM((4, n_exp, 8, tok), jnp.int32),
+            pltpu.VMEM((4, n_exp, 8, tok), F32),
             pltpu.VMEM((tok, width), F32),
             dma((2,)),
         ]
@@ -332,7 +343,7 @@
             bytes_accessed=4 * width * hid,
             transcendentals=8 * tok * hid,
         ),
-    )(tokens, gate_probs, expert_ids, priority[:, None], meta, weight_in, weight_out)
+    )(tokens, gate_probs.T, expert_ids.T, priority[None, :], weight_in, weight_out)
 
 
 def solution(mesh):

time: 89.6 us -> 63.2 us (0.71)
  the two profiles are of different devices: /device:TPU:8 before, /device:TPU:0 now
where the time goes in v2:
time: 63.2 us; the launch traced here: 63.1 us
  Pallas kernels  61.3 us (97%)
  local copies, waits for them, and re-layouts  1.8 us (3%)
    pallas_call x1, Pallas kernels, shards(): pl.pallas_call(functools.partial(kernel, n_exp, base, tok, width), out_sh...  61.3 us
    unnamed x1, local copies, waits for them, and re-layouts  1.8 us

profile of v2, /device:TPU:0, one launch (start us, length us, event | category | flops | bytes accessed | tf_op | source)
XLA Modules:
  0.0 63.1 jit_solution(9834971703908589283)
XLA Ops:
  0.0 61.3 %shard_map.64 = bf16[128,1664]{1,0:T(8,128)(2,1)} custom-call(bf16[128,1664]{1,0:T(8,128)(2,1)} %tokens.1, f32[2,128]{1,0:T(2,128)} %bitcast.3, s32[2,128]{1,0:T(2,128)} %bitcast.4, s32[1,128]{1,0:T(1,128)} %bitcast.5, bf16[1,1664,1024]{2,1,0:T(8,128)(2,1)} %w_in.1, bf16[1,1024,1664]{2,1,0:T(8,128)(2,1)} %w_out.1), custom_call_target="tpu_custom_call" | custom-call | flops 6979321856 | bytes 6815744 | tf_op jit(solution)/shard_map/pallas_call | solution.py:311
  61.3 1.8 %copy.8 = bf16[128,1664]{1,0:T(8,128)(2,1)} copy(bf16[128,1664]{1,0:T(8,128)(2,1)} %shard_map.64) | data formatting | bytes 851968

commit v3 on v2

--- a/solution.py
+++ b/solution.py
@@ -25,6 +25,8 @@
 ):
     tiles = width // 128
     tail = tiles * base
+    cut = tail // 32 * 16
+    halves = ((0, cut), (cut, tail + 16 - cut))
     me = lax.axis_index("expert")
     plane, col = me // 4, me % 4
     sibling = plane * 4 + (col // 2) * 2 + (col + 1) % 2
@@ -54,12 +56,16 @@
     def give_copy(d):
         return remote(give.at[d], got.at[d], g_s.at[d], g_r.at[d], sibling)
 
-    def pair_copy(d):
-        return remote(ysend.at[d], ygot.at[d], y_s.at[d], y_r.at[d], across)
-
-    def return_copy(d):
+    def pair_copy(d, h):
+        span = pl.ds(*halves[h])
         return remote(
-            rsend.at[d], ret.at[n_exp - d], r_s.at[d], r_r.at[n_exp - d], peer(d)
+            ysend.at[d, span], ygot.at[d, span], y_s.at[2 * d + h], y_r.at[2 * d + h], across
+        )
+
+    def return_copy(d, h):
+        span, j = pl.ds(*halves[h]), n_exp - d
+        return remote(
+            rsend.at[d, span], ret.at[j, span], r_s.at[2 * d + h], r_r.at[2 * j + h], peer(d)
         )
 
     def info_copy(j):
@@ -151,9 +157,15 @@
 
     order = (1, 3, 0, 2)
 
-    def finish(d):
-        pair_copy(d).wait_recv()
-        rsend[d] = (keep[d, 0] + ygot[d].astype(F32)).astype(BF16)
+    def finish(d, h):
+        span = pl.ds(*halves[h])
+        pair_copy(d, h).wait_recv()
+        rsend[d, span] = (keep[d, 0, span] + ygot[d, span].astype(F32)).astype(BF16)
+
+    def add_pair(d, h):
+        span = pl.ds(*halves[h])
+        ysend[d, span] = (keep[d, 1, span] + got[d, 1, span].astype(F32)).astype(BF16)
+        pair_copy(d, h).start()
 
     def group(d, c):
         to_across(d).wait_recv()
@@ -203,15 +215,21 @@
 
         @pl.when(d > 0)
         def _():
-            finish(d - 1)
+            finish(d - 1, 0)
+            finish(d - 1, 1)
 
         @pl.when(d > 1)
         def _():
-            return_copy(d - 1).start()
+            return_copy(d - 1, 0).start()
+            return_copy(d - 1, 1).start()
 
         give_copy(d).wait_recv()
-        ysend[d] = (keep[d, 1] + got[d, 1].astype(F32)).astype(BF16)
-        pair_copy(d).start()
+        add_pair(d, 0)
+
+        @pl.when(d < n_exp - 1)
+        def _():
+            add_pair(d, 1)
+
         keep[d, 0] = keep[d, 0] + got[d, 0].astype(F32)
         return c
 
@@ -266,13 +284,18 @@
             acc[:, lanes] += weight * found[:, lanes] + over * last[t : t + 1, :]
 
     acc[...] = jnp.zeros_like(acc)
+    pair_copy(n_exp - 1, 0).wait_send()
+    add_pair(n_exp - 1, 1)
+    finish(n_exp - 1, 0)
+    return_copy(n_exp - 1, 0).start()
     combine(plane, rsend.at[0])
-    finish(n_exp - 1)
-    return_copy(n_exp - 1).start()
+    finish(n_exp - 1, 1)
+    return_copy(n_exp - 1, 1).start()
 
     def collect(i, c):
         j = n_exp - i
-        return_copy(i).wait_recv()
+        return_copy(i, 0).wait_recv()
+        return_copy(i, 1).wait_recv()
         combine((plane + j) % n_exp, ret.at[j])
         return c
 
@@ -284,12 +307,17 @@
         to_sibling(d).wait_send()
         pass_on(d).wait_send()
         give_copy(d).wait_send()
-        pair_copy(d).wait_send()
+        pair_copy(d, 1).wait_send()
+
+        @pl.when(d < n_exp - 1)
+        def _():
+            pair_copy(d, 0).wait_send()
 
         @pl.when(d > 0)
         def _():
             info_copy(d).wait_send()
-            return_copy(d).wait_send()
+            return_copy(d, 0).wait_send()
+            return_copy(d, 1).wait_send()
 
         return c
 
@@ -333,7 +361,9 @@
             pltpu.VMEM((tok, width), F32),
             dma((2,)),
         ]
-        + [dma((n_exp,))] * 16
+        + [dma((n_exp,))] * 10
+        + [dma((2 * n_exp,))] * 4
+        + [dma((n_exp,))] * 2
         + [dma((2,))] * 2,
         compiler_params=pltpu.CompilerParams(
             collective_id=0, has_side_effects=True, vmem_limit_bytes=56 * 1024 * 1024

time: 63.2 us -> 62.3 us (0.986)
  the two profiles are of different devices: /device:TPU:0 before, /device:TPU:8 now
where the time goes in v3:
time: 62.3 us; the launch traced here: 62 us
  Pallas kernels  60.2 us (97%)
  local copies, waits for them, and re-layouts  1.8 us (3%)
    pallas_call x1, Pallas kernels, shards(): pl.pallas_call(functools.partial(kernel, n_exp, base, tok, width), out_sh...  60.2 us
    unnamed x1, local copies, waits for them, and re-layouts  1.8 us

profile of v3, /device:TPU:8, one launch (start us, length us, event | category | flops | bytes accessed | tf_op | source)
XLA Modules:
  0.0 62.0 jit_solution(5189979070611546705)
XLA Ops:
  0.0 60.2 %shard_map.64 = bf16[128,1664]{1,0:T(8,128)(2,1)} custom-call(bf16[128,1664]{1,0:T(8,128)(2,1)} %tokens.1, f32[2,128]{1,0:T(2,128)} %bitcast.3, s32[2,128]{1,0:T(2,128)} %bitcast.4, s32[1,128]{1,0:T(1,128)} %bitcast.5, bf16[1,1664,1024]{2,1,0:T(8,128)(2,1)} %w_in.1, bf16[1,1024,1664]{2,1,0:T(8,128)(2,1)} %w_out.1), custom_call_target="tpu_custom_call" | custom-call | flops 6979321856 | bytes 6815744 | tf_op jit(solution)/shard_map/pallas_call | solution.py:339
  60.2 1.8 %copy.8 = bf16[128,1664]{1,0:T(8,128)(2,1)} copy(bf16[128,1664]{1,0:T(8,128)(2,1)} %shard_map.64) | data formatting | bytes 851968

commit v4 on v3

--- a/solution.py
+++ b/solution.py
@@ -123,6 +123,7 @@
         dst[tail : tail + 16, :] = ext_out[0].astype(BF16)
 
     pack(plane, rows.at[0, 0])
+    pack((plane + n_exp - 1) % n_exp, snd.at[1])
     pl.semaphore_wait(barrier, n_exp + 1)
     to_across(0).start()
     to_sibling(0).start()
@@ -132,17 +133,13 @@
         return c
 
     lax.fori_loop(1, n_exp, start_info, 0)
+    dispatch(1).start()
 
     def pack_send(j, c):
         pack((plane + n_exp - j) % n_exp, snd.at[j])
-
-        @pl.when(j == 1)
-        def _():
-            dispatch(j).start()
-
-        return c
-
-    lax.fori_loop(1, n_exp, pack_send, 0)
+        return c
+
+    lax.fori_loop(2, n_exp, pack_send, 0)
 
     def wait_info(j, c):
         info_copy(j).wait_recv()

time: 62.3 us -> 62.2 us (level)
  no operation moved by 1% of the time
where the time goes in v4:
time: 62.2 us; the launch traced here: 61.8 us
  Pallas kernels  60 us (96%)
  local copies, waits for them, and re-layouts  1.8 us (3%)
    pallas_call x1, Pallas kernels, shards(): pl.pallas_call(functools.partial(kernel, n_exp, base, tok, width), out_sh...  60 us
    unnamed x1, local copies, waits for them, and re-layouts  1.8 us

profile of v4, /device:TPU:8, one launch (start us, length us, event | category | flops | bytes accessed | tf_op | source)
XLA Modules:
  0.0 61.8 jit_solution(11378963477883169739)
XLA Ops:
  0.0 60.0 %shard_map.64 = bf16[128,1664]{1,0:T(8,128)(2,1)} custom-call(bf16[128,1664]{1,0:T(8,128)(2,1)} %tokens.1, f32[2,128]{1,0:T(2,128)} %bitcast.3, s32[2,128]{1,0:T(2,128)} %bitcast.4, s32[1,128]{1,0:T(1,128)} %bitcast.5, bf16[1,1664,1024]{2,1,0:T(8,128)(2,1)} %w_in.1, bf16[1,1024,1664]{2,1,0:T(8,128)(2,1)} %w_out.1), custom_call_target="tpu_custom_call" | custom-call | flops 6979321856 | bytes 6815744 | tf_op jit(solution)/shard_map/pallas_call | solution.py:336
  60.0 1.8 %copy.8 = bf16[128,1664]{1,0:T(8,128)(2,1)} copy(bf16[128,1664]{1,0:T(8,128)(2,1)} %shard_map.64) | data formatting | bytes 851968
